TPU v7x, 32 devices: a whole 2x2x4 slice. The times are simulated.
32 devices in a mesh: groups: 2 (over y), ctx: 4 (over x, core), head: 4 (over z).
Axes of the slice: x: 2, y: 2, z: 4, core: 2. Of those that a mesh axis runs over, the one named last changes fastest.
Arguments:
- queries: bfloat16 [384, 64, 128], P(('groups', 'ctx'), 'head'), parts along dimension 0, may hold values from -16 to 16
- prefix_keys: bfloat16 [16384, 8, 128], P(('groups', 'ctx'), 'head'), parts along dimension 0, may hold values from -16 to 16
- prefix_values: bfloat16 [16384, 8, 128], P(('groups', 'ctx'), 'head'), parts along dimension 0, may hold values from -12 to 12
- suffix_keys: bfloat16 [384, 512, 8, 128], P(('groups', 'ctx'), None, 'head'), parts along dimension 0, may hold values from -16 to 16
- suffix_values: bfloat16 [384, 512, 8, 128], P(('groups', 'ctx'), None, 'head'), parts along dimension 0, may hold values from -12 to 12
- lengths: int32 [384], P(('groups', 'ctx')), parts along dimension 0, may hold values from 1 to 512, as said below
Outputs:
- attended: bfloat16 [384, 64, 128], P(('groups', 'ctx'), 'head'), parts along dimension 0
There are 2 independent parts, one for each index of `groups`. A program takes and returns all parts, laid end to end along the dimension named above; each array names one. Nothing has to cross between parts.
Inputs may be any that keep to these rules, and one draw needn't show every extreme that they name: The live slots of a row are its first lengths[r] slots; some row of each part has exactly 512.
All inputs are finite; a program needn't handle non-finite values.
Results may differ from a plain program's by a relative error of at most 0.0025.
Values may be sent and summed in bfloat16 or wider, within the bound.
No kernel may reach another device: no remote copies, remote signals or barrier semaphores. Data moves between devices by JAX's collectives and lax.ppermute only.
A program may use at most 128 MiB of HBM per device.

v0:
```python
import jax
import jax.numpy as jnp
from jax import lax
from jax.sharding import PartitionSpec as P


def shards(queries, prefix_keys, prefix_values, suffix_keys, suffix_values, lengths):
    rows_dev, heads_local, head_width = queries.shape
    kv_local = prefix_keys.shape[1]
    group_size = heads_local // kv_local
    span = suffix_keys.shape[1]
    scaling = head_width ** (-0.5)
    ctx_count = lax.axis_size("ctx")
    every_query = lax.all_gather(queries, "ctx", axis=0, tiled=True)
    all_rows = every_query.shape[0]
    shards_per = max(1, min(ctx_count, 1024 // max(1, rows_dev * group_size)))
    while ctx_count % shards_per:
        shards_per -= 1
    block_rows = rows_dev * shards_per
    block_count = all_rows // block_rows
    blocked = every_query.reshape(block_count, block_rows, kv_local, group_size, head_width)

    def block_terms(row_block):
        scores = (
            jnp.einsum("rkgd,pkd->rkgp", row_block, prefix_keys, preferred_element_type=jnp.float32)
            * scaling
        )
        local_top = jnp.max(scores, axis=-1)
        weights = jnp.exp(scores - local_top[..., None]).astype(jnp.bfloat16)
        sums_now = jnp.sum(weights, axis=-1, dtype=jnp.float32)
        accum_now = jnp.einsum(
            "rkgp,pkd->rkgd", weights, prefix_values, preferred_element_type=jnp.float32
        )
        return (local_top, sums_now, accum_now)

    prefix_top, prefix_sum, prefix_accum = lax.map(block_terms, blocked)
    prefix_top = prefix_top.reshape(all_rows, kv_local, group_size)
    prefix_sum = prefix_sum.reshape(all_rows, kv_local, group_size)
    prefix_accum = prefix_accum.reshape(all_rows, kv_local, group_size, head_width)
    own_query = queries.reshape(rows_dev, kv_local, group_size, head_width)
    start_row = lax.axis_index("ctx") * rows_dev
    positions = jnp.arange(span, dtype=jnp.int32)
    live_all = (positions[None, :] < lengths[:, None])[:, None, None, :]
    suffix_scores = (
        jnp.einsum("rkgd,rskd->rkgs", own_query, suffix_keys, preferred_element_type=jnp.float32)
        * scaling
    )
    suffix_top = jnp.max(jnp.where(live_all, suffix_scores, -jnp.inf), axis=-1)
    own_prefix_top = lax.dynamic_slice_in_dim(prefix_top, start_row, rows_dev, 0)
    merged_top = lax.dynamic_update_slice_in_dim(
        prefix_top, jnp.maximum(own_prefix_top, suffix_top), start_row, 0
    )
    row_top = lax.pmax(merged_top, "ctx")
    own_top = lax.dynamic_slice_in_dim(row_top, start_row, rows_dev, 0)
    weights = jnp.where(live_all, jnp.exp(suffix_scores - own_top[..., None]), 0.0).astype(
        jnp.bfloat16
    )
    sums_now = jnp.sum(weights, axis=-1, dtype=jnp.float32)
    accum_now = jnp.einsum(
        "rkgs,rskd->rkgd", weights, suffix_values, preferred_element_type=jnp.float32
    )
    block_scale = jnp.exp(prefix_top - row_top)
    prefix_sum = prefix_sum * block_scale
    prefix_accum = prefix_accum * block_scale[..., None]
    full_sum, full_accum = lax.psum((prefix_sum, prefix_accum), "ctx")
    shared_sum = lax.dynamic_slice_in_dim(full_sum, start_row, rows_dev, 0)
    shared_accum = lax.dynamic_slice_in_dim(full_accum, start_row, rows_dev, 0)
    weight_sum = shared_sum + sums_now
    attended = ((shared_accum + accum_now) / weight_sum[..., None]).astype(jnp.bfloat16)
    return attended.reshape(rows_dev, heads_local, head_width)


def solution(mesh):
    placed = (
        P(("groups", "ctx"), "head", None),
        P(("groups", "ctx"), "head", None),
        P(("groups", "ctx"), "head", None),
        P(("groups", "ctx"), None, "head", None),
        P(("groups", "ctx"), None, "head", None),
        P(("groups", "ctx")),
    )
    return jax.shard_map(
        shards,
        mesh=mesh,
        in_specs=placed,
        out_specs=P(("groups", "ctx"), "head", None),
        check_vma=False,
    )
```

profile of v0, /device:TPU:0, one launch (start us, length us, event | category | flops | bytes accessed | tf_op | source)
XLA Modules:
  0.0 136.3 jit_solution(2666634758440160694)
XLA Ops:
  6.5 10.4 %all_gather.3 = bf16[192,16,128]{2,1,0:T(8,128)(2,1)S(1)} all-gather(bf16[48,16,128]{2,1,0:T(8,128)(2,1)} %param.8), channel_id=1, replica_groups=mesh['groups'=2,'ctx'=4,'head'=4] {'ctx'}, dimensions={0}, use_global_device_ids=true | all-gather | bytes 983040 | tf_op jit(solution)/shard_map/all_gather | solution.py:14
  16.9 1.4 copy.38
  18.3 0.1 copy.39
  18.5 39.7 %while.14 = (s32[]{:T(128)}, f32[2,96,2,8]{1,0,3,2:T(2,128)S(1)}, f32[2,96,2,8]{1,0,3,2:T(2,128)S(1)}, f32[2,96,2,8,128]{4,3,2,1,0:T(8,128)}, bf16[2,96,2,8,128]...) while((s32[]{:T(128)}, f32[2,96,2,8]{1,0,3,2:T(2,128)S(1)}, ...), condition=%wide.region_3.4_spmd, body=%wide.region_0.3_spmd.sunk | while | flops 1642066944 | bytes 55255212 | solution.py:36
  18.5 6.4 %bitcast_reduce_fusion.2 = (f32[96,2,8]{2,0,1:T(8,128)S(1)}, f32[2,96,8,2048]{3,2,1,0:T(8,128)}) fusion(bf16[2048,2,128]{2,0,1:T(8,128)(2,1)S(1)} %get-tuple-element.165, bf16[2,96,2,8,128]{4,3,2,1,0:T(8,128)(2,1)S(1)} %get-tuple-element.164, s32[]{:T(128)S(6)} %copy.94), kind=kOutput, calls=%fused_computation.1.clone.1 | convolution fusion | flops 811596288 | bytes 14030852 | tf_op jit(solution)/shard_map/while/body/eval_jaxpr/rkgd,pkd->rkgp/dot_general | solution.py:25
  25.0 6.1 %convert_reduce_fusion.3 = f32[96,2,8]{2,0,1:T(8,128)S(1)} fusion(f32[96,2,8]{2,0,1:T(8,128)S(1)} %get-tuple-element.140, f32[2,96,8,2048]{3,2,1,0:T(8,128)} %get-tuple-element.141), kind=kLoop, calls=%fused_computation.4.clone.1 | loop fusion | flops 15727104 | bytes 12595200 | tf_op jit(solution)/shard_map/while/body/eval_jaxpr/reduce_sum | solution.py:30
  31.3 5.8 %convolution_bitcast_fusion.2 = f32[1,96,2,8,128]{4,3,1,2,0:T(8,128)S(1)} fusion(bf16[2048,2,128]{2,0,1:T(8,128)(2,1)S(1)} %get-tuple-element.166, f32[2,96,8,2048]{3,2,1,0:T(8,128)} %get-tuple-element.141, f32[96,2,8]{2,0,1:T(8,128)S(1)} %get-tuple-element.140), kind=kOutput, calls=%fused_computation.5.clone.1 | convolution fusion | flops 814743552 | bytes 14424064 | tf_op jit(solution)/shard_map/while/body/eval_jaxpr/rkgp,pkd->rkgd/dot_general | solution.py:31
  37.1 1.2 copy-done.1
  38.3 6.4 %bitcast_reduce_fusion.2 = (f32[96,2,8]{2,0,1:T(8,128)S(1)}, f32[2,96,8,2048]{3,2,1,0:T(8,128)}) fusion(bf16[2048,2,128]{2,0,1:T(8,128)(2,1)S(1)} %get-tuple-element.165, bf16[2,96,2,8,128]{4,3,2,1,0:T(8,128)(2,1)S(1)} %get-tuple-element.164, s32[]{:T(128)S(6)} %copy.94), kind=kOutput, calls=%fused_computation.1.clone.1 | convolution fusion | flops 811596288 | bytes 14030852 | tf_op jit(solution)/shard_map/while/body/eval_jaxpr/rkgd,pkd->rkgp/dot_general | solution.py:25
  44.8 6.1 %convert_reduce_fusion.3 = f32[96,2,8]{2,0,1:T(8,128)S(1)} fusion(f32[96,2,8]{2,0,1:T(8,128)S(1)} %get-tuple-element.140, f32[2,96,8,2048]{3,2,1,0:T(8,128)} %get-tuple-element.141), kind=kLoop, calls=%fused_computation.4.clone.1 | loop fusion | flops 15727104 | bytes 12595200 | tf_op jit(solution)/shard_map/while/body/eval_jaxpr/reduce_sum | solution.py:30
  51.1 5.8 %convolution_bitcast_fusion.2 = f32[1,96,2,8,128]{4,3,1,2,0:T(8,128)S(1)} fusion(bf16[2048,2,128]{2,0,1:T(8,128)(2,1)S(1)} %get-tuple-element.166, f32[2,96,8,2048]{3,2,1,0:T(8,128)} %get-tuple-element.141, f32[96,2,8]{2,0,1:T(8,128)S(1)} %get-tuple-element.140), kind=kOutput, calls=%fused_computation.5.clone.1 | convolution fusion | flops 814743552 | bytes 14424064 | tf_op jit(solution)/shard_map/while/body/eval_jaxpr/rkgp,pkd->rkgd/dot_general | solution.py:31
  57.0 1.2 copy-done.1
  58.4 0.1 iota_compare_fusion
  58.5 6.7 %select_reduce_fusion = (f32[48,2,8]{2,1,0:T(2,128)S(1)}, f32[48,2,8,512]{3,2,1,0:T(8,128)S(1)}) fusion(pred[48,512]{1,0:T(8,128)(4,1)S(1)} %iota_compare_fusion, bf16[48,512,2,128]{3,2,1,0:T(2,128)(2,1)} %param.11, bf16[48,16,128]{2,1,0:T(8,128)(2,1)S(1)} %copy-done.4), kind=kOutput, calls=%fused_computation.20 | convolution fusion | flops 101842176 | bytes 14380032 | tf_op jit(solution)/shard_map/rkgd,rskd->rkgs/dot_general | solution.py:45
  65.3 0.2 dynamic_update_slice.14
  65.5 11.2 %pmax.7 = f32[192,2,8]{0,2,1:T(8,128)S(1)} all-reduce(f32[192,2,8]{0,2,1:T(8,128)S(1)} %dynamic_update_slice.14), channel_id=1, replica_groups=mesh['groups'=2,'ctx'=4,'head'=4] {'ctx'}, use_global_device_ids=true, to_apply=%region_5.6 | all-reduce | flops 3072 | bytes 24576 | tf_op jit(solution)/shard_map/pmax | solution.py:53
  76.7 0.2 copy.44
  76.9 1.6 %bitcast_multiply_fusion = f32[192,2,8,128]{3,2,1,0:T(8,128)} fusion(f32[2,96,2,8,128]{4,3,2,1,0:T(8,128)S(1)} %copy-done.2, f32[192,2,8]{2,1,0:T(2,128)S(1)} %copy.44), kind=kLoop, calls=%fused_computation.17 | loop fusion | flops 393216 | bytes 3158016 | tf_op jit(solution)/shard_map/mul | solution.py:64
  78.6 0.1 copy.45
  78.7 0.6 convert_reduce_fusion.1
  79.3 10.6 %psum.15 = f32[192,2,8]{0,2,1:T(8,128)S(1)} all-reduce(f32[192,2,8]{0,2,1:T(8,128)S(1)} %get-tuple-element.89), channel_id=1, replica_groups=mesh['groups'=2,'ctx'=4,'head'=4] {'ctx'}, use_global_device_ids=true, to_apply=%region_7.8 | all-reduce | flops 3072 | bytes 24576 | tf_op jit(solution)/shard_map/psum | solution.py:65
  90.0 0.1 copy.49
  90.1 32.3 %all-reduce.2.cloned.1.call-done = f32[192,2,8,128]{3,2,1,0:T(8,128)} async-done(((f32[192,2,8,128]{3,2,1,0:T(8,128)}), f32[192,2,8,128]{3,2,1,0:T(8,128)}) %all-reduce.2.cloned.1.call-update) | async-done | bytes 1572880 | tf_op jit(solution)/shard_map/psum | solution.py:65
  122.4 7.1 %fusion.20 = bf16[48,16,128]{2,1,0:T(8,128)(2,1)} fusion(bf16[48,512,2,128]{3,2,1,0:T(2,128)(2,1)} %param.12, f32[192,2,8,128]{3,2,1,0:T(8,128)} %all-reduce.2.cloned.1.call-done, s32[]{:T(128)S(6)} %select_n.14, f32[48,2,8]{2,1,0:T(2,128)S(1)} %copy.49, f32[48,2,8,512]{3,2,1,0:T(8,128)S(1)} %get-tuple-element.94, f32[48,2,8]{2,1,0:T(2,128)S(1)} %copy.45, ...), kind=kOutput, calls=%fused_computation.24 | convolution fusion | flops 102531072 | bytes 14776324 | tf_op jit(solution)/shard_map/rkgs,rskd->rkgd/dot_general | solution.py:59
  (38 shorter events, 1.2 us)
Async XLA Ops:
  6.5 115.8 %all-reduce.2.cloned.1.call-start = ((), (), s32[]{:S(2)}) async-start(), calls=%async_computation | async-start | bytes 3145728 | tf_op jit(solution)/shard_map/psum | solution.py:65
  6.5 11.7 %copy-start.3 = (bf16[2048,2,128]{2,1,0:T(2,128)(2,1)S(1)}, bf16[2048,2,128]{2,1,0:T(2,128)(2,1)}, u32[]{:S(2)}) copy-start(bf16[2048,2,128]{2,1,0:T(2,128)(2,1)} %param.10) | copy-start | bytes 3145732
  18.4 39.9 %copy-start.5 = (s32[48]{0:T(128)S(1)}, s32[48]{0:T(128)}, u32[]{:S(2)}) copy-start(s32[48]{0:T(128)} %param.13) | copy-start | bytes 580
  18.4 40.0 %copy-start.4 = (bf16[48,16,128]{2,1,0:T(8,128)(2,1)S(1)}, bf16[48,16,128]{2,1,0:T(8,128)(2,1)}, u32[]{:S(2)}) copy-start(bf16[48,16,128]{2,1,0:T(8,128)(2,1)} %param.8) | copy-start | bytes 589828
  31.2 5.8 %copy-start = (f32[2,96,2,8,128]{4,3,2,1,0:T(8,128)S(1)}, f32[2,96,2,8,128]{4,3,2,1,0:T(8,128)}, u32[]{:S(2)}) copy-start(f32[2,96,2,8,128]{4,3,2,1,0:T(8,128)} %get-tuple-element.154) | copy-start | bytes 4718596 | tf_op jit(solution)/shard_map/while
  37.1 1.2 copy-start.1
  51.1 5.8 %copy-start = (f32[2,96,2,8,128]{4,3,2,1,0:T(8,128)S(1)}, f32[2,96,2,8,128]{4,3,2,1,0:T(8,128)}, u32[]{:S(2)}) copy-start(f32[2,96,2,8,128]{4,3,2,1,0:T(8,128)} %get-tuple-element.154) | copy-start | bytes 4718596 | tf_op jit(solution)/shard_map/while
  57.0 1.2 copy-start.1
  58.5 18.4 %copy-start.2 = (f32[2,96,2,8,128]{4,3,2,1,0:T(8,128)S(1)}, f32[2,96,2,8,128]{4,3,2,1,0:T(8,128)}, u32[]{:S(2)}) copy-start(f32[2,96,2,8,128]{4,3,2,1,0:T(8,128)} %get-tuple-element.44) | copy-start | bytes 4718596
Sparse Core Ops, SparseCore 0:
  78.6 43.6 all-reduce.1
where the time goes:
time: 137 us; the launch traced here: 136 us
  matrix products  38.1 us (28%)
  waiting for transfers between devices  32.3 us (24%)
  blocking collectives  32.1 us (23%)
  other arithmetic  14.7 us (11%)
  between operations  13.5 us (10%)
  local copies, waits for them, and re-layouts  5.44 us (4%)
    psum x1, waiting for transfers between devices, shards(): full_sum, full_accum = lax.psum((prefix_sum, prefix_accum), 'ctx')  32.3 us
    dot_general x2, matrix products, block_terms(): jnp.einsum('rkgd,pkd->rkgp', row_block, prefix_keys, preferred_element_ty...  12.7 us
    reduce_sum x2, other arithmetic, block_terms(): sums_now = jnp.sum(weights, axis=-1, dtype=jnp.float32)  12.3 us
    dot_general x2, matrix products, block_terms(): jnp.einsum('rkgp,pkd->rkgd', weights, prefix_values, preferred_element_ty...  11.6 us
    pmax x1, blocking collectives, shards(): row_top = lax.pmax(merged_top, 'ctx')  11.2 us
    psum x1, blocking collectives, shards(): full_sum, full_accum = lax.psum((prefix_sum, prefix_accum), 'ctx')  10.6 us
    all_gather x1, blocking collectives, shards(): every_query = lax.all_gather(queries, 'ctx', axis=0, tiled=True)  10.4 us
    dot_general x1, matrix products, shards(): jnp.einsum('rkgs,rskd->rkgd', weights, suffix_values, preferred_element_t...  7.14 us
  transfers between devices with their start and end apart: 1, of which 1 were waited for; matrix products, arithmetic and copies ran while one was open for 1% of the time, Pallas kernels for 0%

commit v1 on v0

v1 whole, which is shorter than its diff:
```python
from functools import partial

import jax
import jax.numpy as jnp
from jax import lax
from jax.experimental import pallas as pl
from jax.experimental.pallas import tpu as pltpu
from jax.sharding import PartitionSpec as P

LOG2E = 1.4426950408889634
F32 = jnp.float32
BF16 = jnp.bfloat16
VMEM = pl.BlockSpec(memory_space=pltpu.VMEM)


def split_heads(q_ref, kv_heads):
    rows, heads, d = q_ref.shape
    group = heads // kv_heads
    wide = q_ref[...].astype(F32)
    return [
        wide[:, h * group : (h + 1) * group, :].reshape(rows * group, d).astype(BF16)
        for h in range(kv_heads)
    ]


def block_attend(q, k, v, c):
    s = lax.dot_general(q, k, (((1,), (1,)), ((), ())), preferred_element_type=F32)
    top = jnp.max(s, axis=1, keepdims=True)
    w = jnp.exp2(s * c - top * c).astype(BF16)
    va = jnp.concatenate([v, jnp.ones_like(v)], axis=1)
    oa = jnp.dot(w, va, preferred_element_type=F32)
    d = v.shape[1]
    return oa[:, :d], oa[:, d:], top * c


def attend_blocks(q, blocks, c):
    parts = [block_attend(q, k, v, c) for k, v in blocks]
    top = parts[0][2]
    for part in parts[1:]:
        top = jnp.maximum(top, part[2])
    acc = 0.0
    total = 0.0
    for o, l, t in parts:
        scale = jnp.exp2(t - top)
        acc = acc + o * scale
        total = total + l * scale
    return acc / total, top + jnp.log2(total)


def lane_eye(n):
    return lax.broadcasted_iota(jnp.int32, (n, n), 0) == lax.broadcasted_iota(jnp.int32, (n, n), 1)


def other_kernel(q_ref, *refs, c, kv_heads, pieces):
    kv_refs, msg_ref = refs[:-1], refs[-1]
    heads_q = split_heads(q_ref, kv_heads)
    m, d = heads_q[0].shape
    eye = lane_eye(d)
    packed = []
    for h in range(kv_heads):
        blocks = [(kv_refs[2 * b][h], kv_refs[2 * b + 1][h]) for b in range(len(kv_refs) // 2)]
        o, lse = attend_blocks(heads_q[h], blocks, c)
        msg_ref[h * m : (h + 1) * m, :] = o.astype(BF16)
        packed.append(jnp.sum(jnp.where(eye, lse.reshape(m // d, d, d), 0.0), axis=1))
    rest = jnp.concatenate(packed, axis=0)
    out = []
    for _ in range(3):
        piece = rest.astype(BF16).astype(F32)
        out.append(piece)
        rest = rest - piece
    used = 3 * out[0].shape[0]
    if pieces > used:
        out.append(jnp.zeros((pieces - used, d), F32))
    msg_ref[kv_heads * m :, :] = jnp.concatenate(out, axis=0).astype(BF16)


def own_kernel(q_ref, *refs, c, kv_heads):
    kv_refs, o_ref, lse_ref = refs[:-2], refs[-2], refs[-1]
    heads_q = split_heads(q_ref, kv_heads)
    for h in range(kv_heads):
        blocks = [(kv_refs[2 * b][h], kv_refs[2 * b + 1][h]) for b in range(len(kv_refs) // 2)]
        o, lse = attend_blocks(heads_q[h], blocks, c)
        o_ref[h] = o
        lse_ref[h] = lse


def suffix_kernel(len_ref, q_ref, k_hbm, v_hbm, o_ref, lse_ref, kb, vb, ksem, vsem, *, c, kv_heads, batch):
    rows, heads, d = q_ref.shape
    group = heads // kv_heads
    slots = kb.shape[1]
    lane = lax.broadcasted_iota(jnp.int32, (heads, slots), 1)
    head = lax.broadcasted_iota(jnp.int32, (heads, slots), 0) // group
    place = jnp.where(lane % kv_heads == head, lane // kv_heads, slots)

    def keys(r):
        return pltpu.make_async_copy(k_hbm.at[r], kb.at[r], ksem.at[r])

    def values(r):
        return pltpu.make_async_copy(v_hbm.at[r], vb.at[r], vsem.at[r])

    def issue(r, _):
        keys(r).start()
        values(r).start()
        return 0

    lax.fori_loop(0, rows, issue, 0)

    def body(i, _):
        base = i * batch
        scores = []
        for j in range(batch):
            keys(base + j).wait()
        for j in range(batch):
            r = base + j
            s = lax.dot_general(q_ref[r], kb[r], (((1,), (1,)), ((), ())), preferred_element_type=F32)
            scores.append(jnp.where(place < len_ref[r], s, -jnp.inf))
        weights = []
        for j in range(batch):
            top = jnp.max(scores[j], axis=1, keepdims=True)
            w = jnp.exp2(scores[j] * c - top * c).astype(BF16)
            total = jnp.sum(w.astype(F32), axis=1, keepdims=True)
            weights.append((w, top * c, total))
        for j in range(batch):
            values(base + j).wait()
        for j in range(batch):
            r = base + j
            w, top, total = weights[j]
            o = jnp.dot(w, vb[r], preferred_element_type=F32)
            o_ref[r] = o / total
            lse_ref[r] = jnp.broadcast_to(top + jnp.log2(total), (heads, d))
        return 0

    lax.fori_loop(0, rows // batch, body, 0)


def merge_kernel(os_ref, ls_ref, op_ref, lp_ref, *refs, kv_heads, group):
    msg_refs, out_ref = refs[:-1], refs[-1]
    rows, heads, d = os_ref.shape
    m = rows * group
    n = m // d
    eye = lane_eye(d)
    results = []
    for h in range(kv_heads):
        cols = slice(h * group, (h + 1) * group)
        parts = [
            (os_ref[:, cols, :].reshape(m, d), ls_ref[:, cols, :].reshape(m, d)),
            (op_ref[h], lp_ref[h]),
        ]
        for msg in msg_refs:
            o = msg[h * m : (h + 1) * m, :].astype(F32)
            tail = msg[kv_heads * m :, :].astype(F32)
            lse = sum(tail[(p * kv_heads + h) * n : (p * kv_heads + h + 1) * n] for p in range(3))
            lse = jnp.where(eye, jnp.broadcast_to(lse[:, None, :], (n, d, d)), 0.0)
            lse = jnp.sum(lse, axis=2, keepdims=True).reshape(m, 1)
            parts.append((o, jnp.broadcast_to(lse, (m, d))))
        top = parts[0][1]
        for part in parts[1:]:
            top = jnp.maximum(top, part[1])
        acc = 0.0
        total = 0.0
        for o, l in parts:
            w = jnp.exp2(l - top)
            acc = acc + o * w
            total = total + w
        results.append((acc / total).reshape(rows, group, d))
    out_ref[...] = jnp.concatenate(results, axis=1).astype(BF16)


def shards(queries, prefix_keys, prefix_values, suffix_keys, suffix_values, lengths):
    rows, heads, d = queries.shape
    kv_heads = prefix_keys.shape[1]
    group = heads // kv_heads
    span = suffix_keys.shape[1]
    c = d ** (-0.5) * LOG2E
    n = lax.axis_size("ctx")
    cores = 2 if n % 2 == 0 else 1
    chips = n // cores
    m = rows * group
    pieces = -(-3 * kv_heads * (m // d) // 16) * 16

    def shift(x, by):
        return lax.ppermute(x, "ctx", [(i, (i + by) % n) for i in range(n)])

    def call(kernel, out_shape, operands, specs, scratch=(), mib=40, name=None, flops=0, moved=0):
        single = not isinstance(out_shape, tuple)
        return pl.pallas_call(
            kernel,
            out_shape=out_shape,
            in_specs=specs,
            out_specs=VMEM if single else (VMEM,) * len(out_shape),
            scratch_shapes=scratch,
            compiler_params=pltpu.CompilerParams(vmem_limit_bytes=mib << 20),
            cost_estimate=pl.CostEstimate(flops=flops, bytes_accessed=moved, transcendentals=0),
            name=name,
        )(*operands)

    kv = [(prefix_keys, prefix_values)]
    if cores == 2:
        swap = [(i, i ^ 1) for i in range(n)]
        kv.append((lax.ppermute(prefix_keys, "ctx", swap), lax.ppermute(prefix_values, "ctx", swap)))
    visiting = [shift(queries, j * cores) for j in range(1, chips)]

    slots = span * kv_heads
    suffix_o, suffix_l = call(
        partial(suffix_kernel, c=c, kv_heads=kv_heads, batch=8 if rows % 8 == 0 else 1),
        (jax.ShapeDtypeStruct((rows, heads, d), F32),) * 2,
        (lengths, queries, suffix_keys.reshape(rows, slots, d), suffix_values.reshape(rows, slots, d)),
        [pl.BlockSpec(memory_space=pltpu.SMEM), VMEM, pl.BlockSpec(memory_space=pl.ANY), pl.BlockSpec(memory_space=pl.ANY)],
        scratch=[
            pltpu.VMEM((rows, slots, d), BF16),
            pltpu.VMEM((rows, slots, d), BF16),
            pltpu.SemaphoreType.DMA((rows,)),
            pltpu.SemaphoreType.DMA((rows,)),
        ],
        mib=40,
        name="suffix",
        flops=4 * rows * heads * slots * d,
        moved=4 * rows * slots * d,
    )

    flat = [x.transpose(1, 0, 2) for pair in kv for x in pair]
    positions = cores * prefix_keys.shape[0]
    flops = 4 * m * kv_heads * positions * d
    message = jax.ShapeDtypeStruct((kv_heads * m + pieces, d), BF16)
    returned = []
    for j, q in enumerate(visiting):
        msg = call(
            partial(other_kernel, c=c, kv_heads=kv_heads, pieces=pieces),
            message,
            (q, *flat),
            [VMEM] * (1 + len(flat)),
            name="visiting",
            flops=flops,
            moved=4 * kv_heads * positions * d,
        )
        returned.append(shift(msg, -(j + 1) * cores))
    own_o, own_l = call(
        partial(own_kernel, c=c, kv_heads=kv_heads),
        (jax.ShapeDtypeStruct((kv_heads, m, d), F32),) * 2,
        (queries, *flat),
        [VMEM] * (1 + len(flat)),
        name="own",
        flops=flops,
        moved=4 * kv_heads * positions * d,
    )
    operands = (suffix_o, suffix_l, own_o, own_l, *returned)
    return call(
        partial(merge_kernel, kv_heads=kv_heads, group=group),
        jax.ShapeDtypeStruct((rows, heads, d), BF16),
        operands,
        [VMEM] * len(operands),
        name="merge",
    )


def solution(mesh):
    placed = (
        P(("groups", "ctx"), "head", None),
        P(("groups", "ctx"), "head", None),
        P(("groups", "ctx"), "head", None),
        P(("groups", "ctx"), None, "head", None),
        P(("groups", "ctx"), None, "head", None),
        P(("groups", "ctx")),
    )
    return jax.shard_map(
        shards,
        mesh=mesh,
        in_specs=placed,
        out_specs=P(("groups", "ctx"), "head", None),
        check_vma=False,
    )
```

time: 137 us -> 41.2 us (0.30)
  matrix products: 38.1 us -> 0 us
  blocking collectives: 32.1 us -> 0 us
  waiting for transfers between devices: 32.3 us -> 5.37 us
  Pallas kernels: 0 us -> 21.2 us
  other arithmetic: 14.7 us -> 0 us
  between operations: 13.5 us -> 0.04 us
  starting transfers between devices: 0.01 us -> 5.38 us
  local copies, waits for them, and re-layouts: 5.44 us -> 8.88 us
    dot_general x6 -> x0, matrix products: 38.1 us -> none  [the longest x2 12.7 us: block_terms(): jnp.einsum('rkgd,pkd->rkgp', row_block, prefix_keys, preferred_element_ty...]
    psum x1 -> x0, waiting for transfers between devices: 32.3 us -> none  [shards(): full_sum, full_accum = lax.psum((prefix_sum, prefix_accum), 'ctx')]
    pallas_call x0 -> x4, Pallas kernels: none -> 21.2 us  [call(): pl.pallas_call(kernel, out_shape=out_shape, in_specs=specs, out_specs=VME...]
    reduce_sum x3 -> x0, other arithmetic: 12.9 us -> none  [the longest x2 12.3 us: block_terms(): sums_now = jnp.sum(weights, axis=-1, dtype=jnp.float32)]
    pmax x1 -> x0, blocking collectives: 11.2 us -> none  [shards(): row_top = lax.pmax(merged_top, 'ctx')]
    psum x1 -> x0, blocking collectives: 10.6 us -> none  [shards(): full_sum, full_accum = lax.psum((prefix_sum, prefix_accum), 'ctx')]
    all_gather x1 -> x0, blocking collectives: 10.4 us -> none  [shards(): every_query = lax.all_gather(queries, 'ctx', axis=0, tiled=True)]
    unnamed x9 -> x8, local copies, waits for them, and re-layouts: 0.03 us -> 8.88 us
  transfers between devices with their start and end apart: 1 -> 4, of which waited for: 1 -> 1; matrix products, arithmetic and copies ran while one was open for 1% -> 3% of each run, Pallas kernels for 0% -> 37%
where the time goes in v1:
time: 41.2 us; the launch traced here: 40.9 us
  Pallas kernels  21.2 us (51%)
  local copies, waits for them, and re-layouts  8.88 us (22%)
  starting transfers between devices  5.38 us (13%)
  waiting for transfers between devices  5.37 us (13%)
    pallas_call x4, Pallas kernels, call(): pl.pallas_call(kernel, out_shape=out_shape, in_specs=specs, out_specs=VME...  21.2 us
    unnamed x8, local copies, waits for them, and re-layouts  8.88 us
    ppermute x2, waiting for transfers between devices, shift(): return lax.ppermute(x, 'ctx', [(i, (i + by) % n) for i in range(n)])  5.36 us
    ppermute x2, starting transfers between devices, shift(): return lax.ppermute(x, 'ctx', [(i, (i + by) % n) for i in range(n)])  4.74 us
  transfers between devices with their start and end apart: 4, of which 1 were waited for; matrix products, arithmetic and copies ran while one was open for 3% of the time, Pallas kernels for 37%

profile of v1, /device:TPU:0, one launch (start us, length us, event | category | flops | bytes accessed | tf_op | source)
XLA Modules:
  0.0 40.9 jit_solution(13796709705225298533)
XLA Ops:
  0.0 1.4 %copy.16 = bf16[2048,2,128]{2,0,1:T(8,128)(2,1)S(1)} copy(bf16[2048,2,128]{2,1,0:T(2,128)(2,1)} %param.7) | data formatting | bytes 2097152 | tf_op args[1]
  1.4 0.5 %collective-permute-start = (bf16[2048,2,128]{2,0,1:T(8,128)(2,1)S(1)}, bf16[2048,2,128]{2,0,1:T(8,128)(2,1)S(1)}, u32[]{:S(2)}, u32[]{:S(2)}) collective-permute-start(bf16[2048,2,128]{2,0,1:T(8,128)(2,1)S(1)} %copy.16), channel_id=1, source_target_pairs={{0,4},{4,0},{8,12},{12,8},{1,5},{5,1},{9,13},{13,9},{2,6},{6,2},{1... | collective-permute-start | bytes 3145736 | tf_op jit(solution)/shard_map/ppermute | solution.py:200
  1.9 1.4 %copy.15 = bf16[2048,2,128]{2,0,1:T(8,128)(2,1)S(1)} copy(bf16[2048,2,128]{2,1,0:T(2,128)(2,1)} %param.8) | data formatting | bytes 2097152 | tf_op args[2]
  3.2 0.1 collective-permute-start.1
  3.4 2.9 %collective-permute-start.2 = (bf16[48,16,128]{2,1,0:T(8,128)(2,1)}, bf16[48,16,128]{2,1,0:T(8,128)(2,1)S(1)}, u32[]{:S(2)}, u32[]{:S(2)}) collective-permute-start(bf16[48,16,128]{2,1,0:T(8,128)(2,1)} %q_ref.3), channel_id=1, source_target_pairs={{0,8},{4,12},{8,0},{12,4},{1,9},{5,13},{9,1},{13,5},{2,10},{6,14},... | collective-permute-start | bytes 589832 | tf_op jit(solution)/shard_map/ppermute | solution.py:182
  6.3 5.4 %collective-permute-done.2.q_ref = bf16[48,16,128]{2,1,0:T(8,128)(2,1)S(1)} collective-permute-done((bf16[48,16,128]{2,1,0:T(8,128)(2,1)}, bf16[48,16,128]{2,1,0:T(8,128)(2,1)S(1)}, u32[]{:S(2)}, u32[]{:S(2)}) %collective-permute-start.2) | collective-permute-done | bytes 196640 | tf_op jit(solution)/shard_map/ppermute | solution.py:182
  11.7 0.0 collective-permute-done
  11.7 0.0 collective-permute-done.1
  11.7 5.0 %visiting.1 = bf16[800,128]{1,0:T(8,128)(2,1)S(1)} custom-call(bf16[48,16,128]{2,1,0:T(8,128)(2,1)S(1)} %collective-permute-done.2.q_ref, bf16[2,2048,128]{2,1,0:T(8,128)(2,1)S(1)} %bitcast.9, bf16[2,2048,128]{2,1,0:T(8,128)(2,1)S(1)} %bitcast.11, bf16[2,2048,128]{2,1,0:T(8,128)(2,1)S(1)} %bitcast.13, bf16[2,2048,128]{2,1,0:T(8,128)(2,1)S(1)} %bitcast.15), custom_call_target="tpu_custom_call" | custom-call | flops 1610612736 | bytes 4194304 | tf_op jit(solution)/shard_map/visiting/pallas_call | solution.py:186
  16.7 1.8 %collective-permute-start.3 = (bf16[800,128]{1,0:T(8,128)(2,1)S(1)}, bf16[800,128]{1,0:T(8,128)(2,1)S(1)}, u32[]{:S(2)}, u32[]{:S(2)}) collective-permute-start(bf16[800,128]{1,0:T(8,128)(2,1)S(1)} %visiting.1), channel_id=1, source_target_pairs={{0,8},{4,12},{8,0},{12,4},{1,9},{5,13},{9,1},{13,5},{2,10},{6,14},... | collective-permute-start | bytes 614408 | tf_op jit(solution)/shard_map/ppermute | solution.py:182
  18.5 0.0 copy-start
  18.5 4.6 %copy-done = bf16[48,512,2,128]{3,2,1,0:T(2,128)(2,1)S(1)} copy-done((bf16[48,512,2,128]{3,2,1,0:T(2,128)(2,1)S(1)}, bf16[48,512,2,128]{3,2,1,0:T(2,128)(2,1)}, u32[]{:S(2)}) %copy-start) | copy-done | bytes 12582936
  23.1 0.0 copy-start.1
  23.1 0.9 %copy-done.1 = bf16[48,16,128]{2,1,0:T(8,128)(2,1)S(1)} copy-done((bf16[48,16,128]{2,1,0:T(8,128)(2,1)S(1)}, bf16[48,16,128]{2,1,0:T(8,128)(2,1)}, u32[]{:S(2)}) %copy-start.1) | copy-done | bytes 196632
  24.0 0.0 copy-start.2
  24.0 0.7 %copy-done.2 = s32[48]{0:T(128)S(1)} copy-done((s32[48]{0:T(128)S(1)}, s32[48]{0:T(128)}, u32[]{:S(2)}) %copy-start.2) | copy-done | bytes 216
  24.6 10.2 %suffix.1 = (f32[48,16,128]{2,1,0:T(8,128)S(1)}, f32[48,16,128]{2,1,0:T(8,128)S(1)}) custom-call(s32[48]{0:T(128)S(1)} %copy-done.2, bf16[48,16,128]{2,1,0:T(8,128)(2,1)S(1)} %copy-done.1, bf16[48,1024,128]{2,1,0:T(8,128)(2,1)S(1)} %bitcast.8, bf16[48,1024,128]{2,1,0:T(8,128)(2,1)} %bitcast.17), custom_call_target="tpu_custom_call" | custom-call | flops 402653184 | bytes 25165824 | tf_op jit(solution)/shard_map/suffix/pallas_call | solution.py:186
  34.9 5.0 %own.1 = (f32[2,384,128]{2,1,0:T(8,128)S(1)}, f32[2,384,128]{2,1,0:T(8,128)S(1)}) custom-call(bf16[48,16,128]{2,1,0:T(8,128)(2,1)S(1)} %copy-done.1, bf16[2,2048,128]{2,1,0:T(8,128)(2,1)S(1)} %bitcast.10, bf16[2,2048,128]{2,1,0:T(8,128)(2,1)S(1)} %bitcast.12, bf16[2,2048,128]{2,1,0:T(8,128)(2,1)S(1)} %bitcast.14, bf16[2,2048,128]{2,1,0:T(8,128)(2,1)S(1)} %bitcast.16), custom_call_target="tpu_custom_call" | custom-call | flops 1610612736 | bytes 4194304 | tf_op jit(solution)/shard_map/own/pallas_call | solution.py:186
  39.9 0.0 collective-permute-done.3.refs_0_
  39.9 1.0 %merge.1 = bf16[48,16,128]{2,1,0:T(8,128)(2,1)} custom-call(f32[48,16,128]{2,1,0:T(8,128)S(1)} %get-tuple-element.9.os_ref, f32[48,16,128]{2,1,0:T(8,128)S(1)} %get-tuple-element.10.ls_ref, f32[2,384,128]{2,1,0:T(8,128)S(1)} %get-tuple-element.11.op_ref, f32[2,384,128]{2,1,0:T(8,128)S(1)} %get-tuple-element.12.lp_ref, ...), custom_call_target="tpu_custom_call" | custom-call | tf_op jit(solution)/shard_map/merge/pallas_call | solution.py:186
Async XLA Ops:
  1.4 10.3 %collective-permute-start = (bf16[2048,2,128]{2,0,1:T(8,128)(2,1)S(1)}, bf16[2048,2,128]{2,0,1:T(8,128)(2,1)S(1)}, u32[]{:S(2)}, u32[]{:S(2)}) collective-permute-start(bf16[2048,2,128]{2,0,1:T(8,128)(2,1)S(1)} %copy.16), channel_id=1, source_target_pairs={{0,4},{4,0},{8,12},{12,8},{1,5},{5,1},{9,13},{13,9},{2,6},{6,2},{1... | collective-permute-start | bytes 3145736 | tf_op jit(solution)/shard_map/ppermute | solution.py:200
  3.2 8.4 %collective-permute-start.1 = (bf16[2048,2,128]{2,0,1:T(8,128)(2,1)S(1)}, bf16[2048,2,128]{2,0,1:T(8,128)(2,1)S(1)}, u32[]{:S(2)}, u32[]{:S(2)}) collective-permute-start(bf16[2048,2,128]{2,0,1:T(8,128)(2,1)S(1)} %copy.15), channel_id=1, source_target_pairs={{0,4},{4,0},{8,12},{12,8},{1,5},{5,1},{9,13},{13,9},{2,6},{6,2},{1... | collective-permute-start | bytes 3145736 | tf_op jit(solution)/shard_map/ppermute | solution.py:200
  3.4 8.3 %collective-permute-start.2 = (bf16[48,16,128]{2,1,0:T(8,128)(2,1)}, bf16[48,16,128]{2,1,0:T(8,128)(2,1)S(1)}, u32[]{:S(2)}, u32[]{:S(2)}) collective-permute-start(bf16[48,16,128]{2,1,0:T(8,128)(2,1)} %q_ref.3), channel_id=1, source_target_pairs={{0,8},{4,12},{8,0},{12,4},{1,9},{5,13},{9,1},{13,5},{2,10},{6,14},... | collective-permute-start | bytes 589832 | tf_op jit(solution)/shard_map/ppermute | solution.py:182
  16.7 23.2 %collective-permute-start.3 = (bf16[800,128]{1,0:T(8,128)(2,1)S(1)}, bf16[800,128]{1,0:T(8,128)(2,1)S(1)}, u32[]{:S(2)}, u32[]{:S(2)}) collective-permute-start(bf16[800,128]{1,0:T(8,128)(2,1)S(1)} %visiting.1), channel_id=1, source_target_pairs={{0,8},{4,12},{8,0},{12,4},{1,9},{5,13},{9,1},{13,5},{2,10},{6,14},... | collective-permute-start | bytes 614408 | tf_op jit(solution)/shard_map/ppermute | solution.py:182
  18.5 4.6 %copy-start = (bf16[48,512,2,128]{3,2,1,0:T(2,128)(2,1)S(1)}, bf16[48,512,2,128]{3,2,1,0:T(2,128)(2,1)}, u32[]{:S(2)}) copy-start(bf16[48,512,2,128]{3,2,1,0:T(2,128)(2,1)} %param.9) | copy-start | bytes 37748740
  23.1 0.9 %copy-start.1 = (bf16[48,16,128]{2,1,0:T(8,128)(2,1)S(1)}, bf16[48,16,128]{2,1,0:T(8,128)(2,1)}, u32[]{:S(2)}) copy-start(bf16[48,16,128]{2,1,0:T(8,128)(2,1)} %q_ref.3) | copy-start | bytes 589828
  24.0 0.7 %copy-start.2 = (s32[48]{0:T(128)S(1)}, s32[48]{0:T(128)}, u32[]{:S(2)}) copy-start(s32[48]{0:T(128)} %len_ref.1) | copy-start | bytes 580

commit v2 on v1

--- a/solution.py
+++ b/solution.py
@@ -194,10 +194,10 @@
             name=name,
         )(*operands)
 
-    kv = [(prefix_keys, prefix_values)]
+    flat = [prefix_keys.reshape(-1, d), prefix_values.reshape(-1, d)]
     if cores == 2:
         swap = [(i, i ^ 1) for i in range(n)]
-        kv.append((lax.ppermute(prefix_keys, "ctx", swap), lax.ppermute(prefix_values, "ctx", swap)))
+        flat += [lax.ppermute(x, "ctx", swap) for x in flat]
     visiting = [shift(queries, j * cores) for j in range(1, chips)]
 
     slots = span * kv_heads
@@ -212,13 +212,14 @@
             pltpu.SemaphoreType.DMA((rows,)),
             pltpu.SemaphoreType.DMA((rows,)),
         ],
-        mib=40,
+        mib=50,
         name="suffix",
         flops=4 * rows * heads * slots * d,
         moved=4 * rows * slots * d,
     )
 
-    flat = [x.transpose(1, 0, 2) for pair in kv for x in pair]
+    visiting, flat, suffix_o, suffix_l = lax.optimization_barrier((visiting, flat, suffix_o, suffix_l))
+    flat = [x.reshape(-1, kv_heads, d).transpose(1, 0, 2) for x in flat]
     positions = cores * prefix_keys.shape[0]
     flops = 4 * m * kv_heads * positions * d
     message = jax.ShapeDtypeStruct((kv_heads * m + pieces, d), BF16)

time: 41.2 us -> 29.6 us (0.72)
  local copies, waits for them, and re-layouts: 8.88 us -> 2.17 us
  waiting for transfers between devices: 5.37 us -> 1.84 us
  starting transfers between devices: 5.38 us -> 3.52 us
  Pallas kernels: 21.2 us -> 21.8 us
    unnamed x8, local copies, waits for them, and re-layouts: 8.88 us -> 1.62 us
    ppermute x2, waiting for transfers between devices: 5.36 us -> 1.84 us  [shift(): return lax.ppermute(x, 'ctx', [(i, (i + by) % n) for i in range(n)])]
    ppermute x2, starting transfers between devices: 4.74 us -> 3.01 us  [shift(): return lax.ppermute(x, 'ctx', [(i, (i + by) % n) for i in range(n)])]
    pallas_call x4, Pallas kernels: 21.2 us -> 21.8 us  [call(): pl.pallas_call(kernel, out_shape=out_shape, in_specs=specs, out_specs=VME...]
    transpose x0 -> x2, local copies, waits for them, and re-layouts: none -> 0.55 us  [shards(): flat = [x.reshape(-1, kv_heads, d).transpose(1, 0, 2) for x in flat]]
  transfers between devices with their start and end apart: 4 -> 4, of which waited for: 1 -> 1; matrix products, arithmetic and copies ran while one was open for 3% -> 0% of each run, Pallas kernels for 37% -> 54%
where the time goes in v2:
time: 29.6 us; the launch traced here: 29.4 us
  Pallas kernels  21.8 us (74%)
  starting transfers between devices  3.52 us (12%)
  local copies, waits for them, and re-layouts  2.17 us (7%)
  waiting for transfers between devices  1.84 us (6%)
    pallas_call x4, Pallas kernels, call(): pl.pallas_call(kernel, out_shape=out_shape, in_specs=specs, out_specs=VME...  21.8 us
    ppermute x2, starting transfers between devices, shift(): return lax.ppermute(x, 'ctx', [(i, (i + by) % n) for i in range(n)])  3.01 us
    ppermute x2, waiting for transfers between devices, shift(): return lax.ppermute(x, 'ctx', [(i, (i + by) % n) for i in range(n)])  1.84 us
    unnamed x8, local copies, waits for them, and re-layouts  1.62 us
  transfers between devices with their start and end apart: 4, of which 1 were waited for; matrix products, arithmetic and copies ran while one was open for 0% of the time, Pallas kernels for 54%

profile of v2, /device:TPU:0, one launch (start us, length us, event | category | flops | bytes accessed | tf_op | source)
XLA Modules:
  0.0 29.4 jit_solution(16638063182681129656)
XLA Ops:
  0.0 0.5 %collective-permute-start.1 = (bf16[4096,128]{1,0:T(8,128)(2,1)}, bf16[4096,128]{1,0:T(8,128)(2,1)S(1)}, u32[]{:S(2)}, u32[]{:S(2)}) collective-permute-start(bf16[4096,128]{1,0:T(8,128)(2,1)} %bitcast.19), channel_id=1, source_target_pairs={{0,4},{4,0},{8,12},{12,8},{1,5},{5,1},{9,13},{13,9},{2,6},{6,2},{1... | collective-permute-start | bytes 3145736 | tf_op jit(solution)/shard_map/ppermute | solution.py:200
  0.5 0.1 collective-permute-start.2
  0.5 2.9 %collective-permute-start = (bf16[48,16,128]{2,1,0:T(8,128)(2,1)}, bf16[48,16,128]{2,1,0:T(8,128)(2,1)S(1)}, u32[]{:S(2)}, u32[]{:S(2)}) collective-permute-start(bf16[48,16,128]{2,1,0:T(8,128)(2,1)} %q_ref.3), channel_id=1, source_target_pairs={{0,8},{4,12},{8,0},{12,4},{1,9},{5,13},{9,1},{13,5},{2,10},{6,14},... | collective-permute-start | bytes 589832 | tf_op jit(solution)/shard_map/ppermute | solution.py:182
  3.5 0.0 copy-start
  3.5 1.0 %copy-done = bf16[48,16,128]{2,1,0:T(8,128)(2,1)S(1)} copy-done((bf16[48,16,128]{2,1,0:T(8,128)(2,1)S(1)}, bf16[48,16,128]{2,1,0:T(8,128)(2,1)}, u32[]{:S(2)}) %copy-start) | copy-done | bytes 196632
  4.4 0.0 copy-start.1
  4.4 0.7 %copy-done.1 = s32[48]{0:T(128)S(1)} copy-done((s32[48]{0:T(128)S(1)}, s32[48]{0:T(128)}, u32[]{:S(2)}) %copy-start.1) | copy-done | bytes 216
  5.1 0.0 copy-start.2
  5.1 0.0 copy-start.3
  5.1 11.1 %suffix.1 = (f32[48,16,128]{2,1,0:T(8,128)S(1)}, f32[48,16,128]{2,1,0:T(8,128)S(1)}) custom-call(s32[48]{0:T(128)S(1)} %copy-done.1, bf16[48,16,128]{2,1,0:T(8,128)(2,1)S(1)} %copy-done, bf16[48,1024,128]{2,1,0:T(8,128)(2,1)} %bitcast.16, bf16[48,1024,128]{2,1,0:T(8,128)(2,1)} %bitcast.17), custom_call_target="tpu_custom_call" | custom-call | flops 402653184 | bytes 25165824 | tf_op jit(solution)/shard_map/suffix/pallas_call | solution.py:186
  16.1 0.0 collective-permute-done.q_ref
  16.1 0.0 collective-permute-done.1
  16.2 0.0 collective-permute-done.2
  16.2 0.3 copy_bitcast_fusion
  16.4 0.0 copy-done.2
  16.5 0.0 copy-done.3
  16.5 0.3 copy_bitcast_fusion.2
  16.7 4.9 %visiting.1 = bf16[800,128]{1,0:T(8,128)(2,1)S(1)} custom-call(bf16[48,16,128]{2,1,0:T(8,128)(2,1)S(1)} %collective-permute-done.q_ref, bf16[2,2048,128]{2,1,0:T(8,128)(2,1)S(1)} %get-tuple-element.30.refs_0_, bf16[2,2048,128]{2,1,0:T(8,128)(2,1)S(1)} %get-tuple-element.29.refs_1_, bf16[2,2048,128]{2,1,0:T(8,128)(2,1)S(1)} %get-tuple-element.28.refs_2_, ...), custom_call_target="tpu_custom_call" | custom-call | flops 1610612736 | bytes 4194304 | tf_op jit(solution)/shard_map/visiting/pallas_call | solution.py:186
  21.6 0.1 collective-permute-start.3
  21.7 4.8 %own.1 = (f32[2,384,128]{2,1,0:T(8,128)S(1)}, f32[2,384,128]{2,1,0:T(8,128)S(1)}) custom-call(bf16[48,16,128]{2,1,0:T(8,128)(2,1)S(1)} %copy-done, bf16[2,2048,128]{2,1,0:T(8,128)(2,1)S(1)} %get-tuple-element.30.refs_0_, bf16[2,2048,128]{2,1,0:T(8,128)(2,1)S(1)} %get-tuple-element.29.refs_1_, bf16[2,2048,128]{2,1,0:T(8,128)(2,1)S(1)} %get-tuple-element.28.refs_2_, ...), custom_call_target="tpu_custom_call" | custom-call | flops 1610612736 | bytes 4194304 | tf_op jit(solution)/shard_map/own/pallas_call | solution.py:186
  26.6 1.8 %collective-permute-done.3.refs_0_ = bf16[800,128]{1,0:T(8,128)(2,1)S(1)} collective-permute-done((bf16[800,128]{1,0:T(8,128)(2,1)S(1)}, bf16[800,128]{1,0:T(8,128)(2,1)S(1)}, u32[]{:S(2)}, u32[]{:S(2)}) %collective-permute-start.3) | collective-permute-done | bytes 204832 | tf_op jit(solution)/shard_map/ppermute | solution.py:182
  28.4 1.0 %merge.1 = bf16[48,16,128]{2,1,0:T(8,128)(2,1)} custom-call(f32[48,16,128]{2,1,0:T(8,128)S(1)} %get-tuple-element.18.os_ref, f32[48,16,128]{2,1,0:T(8,128)S(1)} %get-tuple-element.19.ls_ref, f32[2,384,128]{2,1,0:T(8,128)S(1)} %get-tuple-element.24.op_ref, f32[2,384,128]{2,1,0:T(8,128)S(1)} %get-tuple-element.25.lp_ref, ...), custom_call_target="tpu_custom_call" | custom-call | tf_op jit(solution)/shard_map/merge/pallas_call | solution.py:186
Async XLA Ops:
  0.0 16.1 %collective-permute-start.1 = (bf16[4096,128]{1,0:T(8,128)(2,1)}, bf16[4096,128]{1,0:T(8,128)(2,1)S(1)}, u32[]{:S(2)}, u32[]{:S(2)}) collective-permute-start(bf16[4096,128]{1,0:T(8,128)(2,1)} %bitcast.19), channel_id=1, source_target_pairs={{0,4},{4,0},{8,12},{12,8},{1,5},{5,1},{9,13},{13,9},{2,6},{6,2},{1... | collective-permute-start | bytes 3145736 | tf_op jit(solution)/shard_map/ppermute | solution.py:200
  0.5 15.7 %collective-permute-start.2 = (bf16[4096,128]{1,0:T(8,128)(2,1)}, bf16[4096,128]{1,0:T(8,128)(2,1)S(1)}, u32[]{:S(2)}, u32[]{:S(2)}) collective-permute-start(bf16[4096,128]{1,0:T(8,128)(2,1)} %bitcast.18), channel_id=1, source_target_pairs={{0,4},{4,0},{8,12},{12,8},{1,5},{5,1},{9,13},{13,9},{2,6},{6,2},{1... | collective-permute-start | bytes 3145736 | tf_op jit(solution)/shard_map/ppermute | solution.py:200
  0.5 15.6 %collective-permute-start = (bf16[48,16,128]{2,1,0:T(8,128)(2,1)}, bf16[48,16,128]{2,1,0:T(8,128)(2,1)S(1)}, u32[]{:S(2)}, u32[]{:S(2)}) collective-permute-start(bf16[48,16,128]{2,1,0:T(8,128)(2,1)} %q_ref.3), channel_id=1, source_target_pairs={{0,8},{4,12},{8,0},{12,4},{1,9},{5,13},{9,1},{13,5},{2,10},{6,14},... | collective-permute-start | bytes 589832 | tf_op jit(solution)/shard_map/ppermute | solution.py:182
  3.5 1.0 %copy-start = (bf16[48,16,128]{2,1,0:T(8,128)(2,1)S(1)}, bf16[48,16,128]{2,1,0:T(8,128)(2,1)}, u32[]{:S(2)}) copy-start(bf16[48,16,128]{2,1,0:T(8,128)(2,1)} %q_ref.3) | copy-start | bytes 589828
  4.4 0.7 %copy-start.1 = (s32[48]{0:T(128)S(1)}, s32[48]{0:T(128)}, u32[]{:S(2)}) copy-start(s32[48]{0:T(128)} %len_ref.1) | copy-start | bytes 580
  5.1 11.4 %copy-start.2 = (bf16[2048,2,128]{2,1,0:T(2,128)(2,1)S(1)}, bf16[2048,2,128]{2,1,0:T(2,128)(2,1)}, u32[]{:S(2)}) copy-start(bf16[2048,2,128]{2,1,0:T(2,128)(2,1)} %param.8) | copy-start | bytes 3145732
  5.1 11.4 %copy-start.3 = (bf16[2048,2,128]{2,1,0:T(2,128)(2,1)S(1)}, bf16[2048,2,128]{2,1,0:T(2,128)(2,1)}, u32[]{:S(2)}) copy-start(bf16[2048,2,128]{2,1,0:T(2,128)(2,1)} %param.7) | copy-start | bytes 3145732
  21.6 6.8 %collective-permute-start.3 = (bf16[800,128]{1,0:T(8,128)(2,1)S(1)}, bf16[800,128]{1,0:T(8,128)(2,1)S(1)}, u32[]{:S(2)}, u32[]{:S(2)}) collective-permute-start(bf16[800,128]{1,0:T(8,128)(2,1)S(1)} %visiting.1), channel_id=1, source_target_pairs={{0,8},{4,12},{8,0},{12,4},{1,9},{5,13},{9,1},{13,5},{2,10},{6,14},... | collective-permute-start | bytes 614408 | tf_op jit(solution)/shard_map/ppermute | solution.py:182
